TPU v7x, 256 devices: a whole 4x4x8 slice. The times are simulated.
256 devices in a mesh: ell: 32 (over x, y, core), rad: 8 (over z).
Axes of the slice: x: 4, y: 4, z: 8, core: 2. Of those that a mesh axis runs over, the one named last changes fastest.
Arguments:
- shells: bfloat16 [1024, 1024, 128], P('ell', 'rad'), may hold values from -6 to 6
- start_values: float32 [1024, 1024], P('ell', 'rad'), may hold values from 0.01 to 0.09
- rec_scale: float32 [1024, 512], P('ell'), may hold values from 1.7 to 1.9
- rec_shift: float32 [1024, 512], P('ell'), may hold values from -0.05 to 0.05
- rec_damp: float32 [1024, 512], P('ell'), may hold values from 0.996 to 1
- degree_counts: int32 [1024], P('ell'), may hold values from 1 to 512
- owners: int32 [1024], P('ell'), may hold values from 0 to 31, as said below
Outputs:
- coefficients: float32 [1024, 512, 128], P('ell', 'rad')
Inputs may be any that keep to these rules, and one draw needn't show every extreme that they name: `owners`: in every run of 32 ells that starts at a multiple of 32, every owner index appears exactly 1 times.
All inputs are finite; a program needn't handle non-finite values.
Results may differ from a plain program's by a relative error of at most 0.0018.
The roundings to bfloat16 on the way count: a program that leaves them out, or rounds other values in their place, can miss the bound.
Values may be sent and summed in bfloat16 or wider, within the bound.
A program may use at most 64 MiB of HBM per device.

v0:
```python
import jax
import jax.numpy as jnp
from jax import lax
from jax.sharding import PartitionSpec as P

R = 1024


def local_nodes(count_r):
    offset = lax.axis_index("rad") * count_r
    index = (lax.iota(jnp.int32, count_r) + offset).astype(jnp.float32)
    return jnp.cos(jnp.pi * (2.0 * index + 1.0) / (2.0 * R))


def build_tables(start_values, rec_scale, rec_shift, rec_damp, degree_counts, nodes):
    ndeg = rec_scale.shape[1]
    second = rec_scale[:, 0:1] * (nodes[None, :] + rec_shift[:, 0:1]) * start_values

    def advance(carry, inputs):
        previous, current = carry
        scale, shift, damp = inputs
        upcoming = (
            scale[:, None] * (nodes[None, :] + shift[:, None]) * current - damp[:, None] * previous
        )
        return ((current, upcoming), upcoming)

    rest = lax.scan(
        advance,
        (start_values, second),
        (rec_scale[:, 1 : ndeg - 1].T, rec_shift[:, 1 : ndeg - 1].T, rec_damp[:, 1 : ndeg - 1].T),
        unroll=8,
    )[1]
    tables = jnp.concatenate([start_values[None], second[None], rest], axis=0)
    degree = lax.iota(jnp.int32, ndeg)
    live = degree[:, None] < degree_counts[None, :]
    tables = jnp.where(live[:, :, None], tables, jnp.zeros_like(tables))
    return tables.astype(jnp.bfloat16)


def local_partials(shells, start_values, rec_scale, rec_shift, rec_damp, degree_counts):
    nodes = local_nodes(shells.shape[1])
    tables = build_tables(start_values, rec_scale, rec_shift, rec_damp, degree_counts, nodes)
    return jnp.einsum("nei,eic->enc", tables, shells, preferred_element_type=jnp.float32)


def slab_order(owners):
    owned = owners.shape[0]
    share = owned // lax.axis_size("ell")
    same = owners[:, None] == owners[None, :]
    position = lax.iota(jnp.int32, owned)
    before = position[None, :] < position[:, None]
    rank = jnp.sum(jnp.logical_and(same, before).astype(jnp.int32), axis=1)
    return jnp.argsort(owners * share + rank)


def radial_total(partial_value):
    return lax.psum_scatter(partial_value, "rad", scatter_dimension=1, tiled=True)


def body(shells, start_values, rec_scale, rec_shift, rec_damp, degree_counts, owners):
    order = slab_order(owners)
    partial_value = local_partials(
        shells, start_values, rec_scale, rec_shift, rec_damp, degree_counts
    )
    summed = radial_total(partial_value)
    return lax.all_to_all(summed[order], "ell", split_axis=0, concat_axis=0, tiled=True)


def solution(mesh):
    return jax.shard_map(
        body,
        mesh=mesh,
        in_specs=(
            P("ell", "rad", None),
            P("ell", "rad"),
            P("ell", None),
            P("ell", None),
            P("ell", None),
            P("ell"),
            P("ell"),
        ),
        out_specs=P("ell", "rad", None),
        check_vma=False,
    )
```

profile of v0, /device:TPU:1, one launch (start us, length us, event | category | flops | bytes accessed | tf_op | source)
XLA Modules:
  0.0 282.0 jit_solution(5290028673674899502)
XLA Ops:
  6.5 1.0 slice_bitcast_fusion.25
  7.5 0.9 slice_reduce_fusion.18
  8.4 0.9 slice_bitcast_fusion.26
  9.3 0.9 slice_bitcast_fusion.24
  10.3 0.7 copy.53
  11.0 0.8 multiply_multiply_fusion
  12.9 97.9 %while.15 = (s32[]{:T(128)}, f32[32,128]{1,0:T(8,128)S(1)}, f32[32,128]{1,0:T(8,128)S(1)}, bf16[63,8,32,128]{3,2,1,0:T(8,128)(2,1)}, f32[63,8,32]{2,1,0:T(8,128)...) while((s32[]{:T(128)}, f32[32,128]{1,0:T(8,128)S(1)}, ...), condition=%wide.region_1.0_spmd.clone, body=%wide.region_0.0_spmd.clone.sunk | while | flops 307841 | bytes 678377 | solution.py:27
  13.8 0.6 bitcast_dynamic-update-slice_fusion.2
  17.0 0.6 bitcast_dynamic-update-slice_fusion.2
  18.5 0.6 bitcast_dynamic-update-slice_fusion.2
  21.6 0.6 bitcast_dynamic-update-slice_fusion.2
  23.2 0.6 bitcast_dynamic-update-slice_fusion.2
  26.3 0.6 bitcast_dynamic-update-slice_fusion.2
  27.8 0.6 bitcast_dynamic-update-slice_fusion.2
  29.4 0.6 bitcast_dynamic-update-slice_fusion.2
  34.0 0.6 bitcast_dynamic-update-slice_fusion.2
  35.6 0.6 bitcast_dynamic-update-slice_fusion.2
  37.2 0.6 bitcast_dynamic-update-slice_fusion.2
  41.8 0.6 bitcast_dynamic-update-slice_fusion.2
  46.5 0.6 bitcast_dynamic-update-slice_fusion.2
  48.0 0.6 bitcast_dynamic-update-slice_fusion.2
  52.7 0.6 bitcast_dynamic-update-slice_fusion.2
  55.8 0.6 bitcast_dynamic-update-slice_fusion.2
  57.4 0.6 bitcast_dynamic-update-slice_fusion.2
  58.9 0.6 bitcast_dynamic-update-slice_fusion.2
  60.5 0.6 bitcast_dynamic-update-slice_fusion.2
  62.0 0.6 bitcast_dynamic-update-slice_fusion.2
  63.6 0.6 bitcast_dynamic-update-slice_fusion.2
  68.2 0.6 bitcast_dynamic-update-slice_fusion.2
  71.3 0.6 bitcast_dynamic-update-slice_fusion.2
  74.4 0.6 bitcast_dynamic-update-slice_fusion.2
  80.6 0.6 bitcast_dynamic-update-slice_fusion.2
  85.3 0.6 bitcast_dynamic-update-slice_fusion.2
  88.4 0.6 bitcast_dynamic-update-slice_fusion.2
  90.0 0.6 bitcast_dynamic-update-slice_fusion.2
  91.5 0.6 bitcast_dynamic-update-slice_fusion.2
  94.6 0.6 bitcast_dynamic-update-slice_fusion.2
  103.9 0.6 bitcast_dynamic-update-slice_fusion.2
  110.2 0.6 bitcast_dynamic-update-slice_fusion.2
  110.8 5.7 %copy.37 = bf16[504,32,128]{2,0,1:T(8,128)(2,1)} copy(bf16[504,32,128]{2,1,0:T(8,128)(2,1)} %bitcast.128) | data formatting | bytes 8257536 | tf_op jit(solution)/shard_map/reshape | solution.py:27
  116.8 25.2 %concatenate.6 = bf16[512,32,128]{2,0,1:T(8,128)(2,1)} concatenate(f32[1,32,128]{2,0,1:T(1,128)S(1)} %bitcast.135, f32[1,32,128]{2,0,1:T(1,128)S(1)} %bitcast.136, bf16[504,32,128]{2,0,1:T(8,128)(2,1)} %copy.37, f32[1,32,128]{2,0,1:T(1,128)S(1)} %bitcast.142, f32[1,32,128]{2,0,1:T(1,128)S(1)} %bitcast.141, f32[1,32,128]{2,0,1:T(1,128)S(1)} %bitcast.140, ...), dimensions={0} | concatenate | bytes 8454144 | tf_op jit(solution)/shard_map/concatenate | solution.py:33
  142.0 7.1 %fusion.2 = f32[32,512,128]{2,1,0:T(8,128)} fusion(bf16[32,128,128]{2,1,0:T(8,128)(2,1)S(1)} %copy-done, bf16[512,32,128]{2,0,1:T(8,128)(2,1)} %concatenate.6, pred[512,32]{0,1:T(8,128)(4,1)S(1)} %iota_compare_fusion), kind=kOutput, calls=%fused_computation.48 | convolution fusion | flops 538968064 | bytes 13647872 | tf_op jit(solution)/shard_map/nei,eic->enc/dot_general | solution.py:43
  149.1 0.6 copy-done.3
  150.0 1.6 sort.17
  151.6 96.5 %reduce-scatter.2.cloned.1.call-done = f32[32,64,128]{2,1,0:T(8,128)} async-done(((f32[32,512,128]{2,1,0:T(8,128)}), f32[32,64,128]{2,1,0:T(8,128)}) %reduce-scatter.2.cloned.1.call-update) | async-done | bytes 1048592 | tf_op jit(solution)/shard_map/reduce_scatter | solution.py:57
  248.1 1.8 gather_fusion
  250.0 24.2 %all_to_all.5 = f32[32,64,128]{2,1,0:T(8,128)S(1)} all-to-all(f32[32,64,128]{2,1,0:T(8,128)S(1)} %gather_fusion), channel_id=1, replica_groups=mesh['ell'=32,'rad'=8] {'ell'}, dimensions={0} | all-to-all | bytes 2097152 | tf_op jit(solution)/shard_map/all_to_all | solution.py:66
  274.1 1.0 copy.67
  (937 shorter events, 75.4 us)
Async XLA Ops:
  6.5 135.4 %copy-start = (bf16[32,128,128]{2,1,0:T(8,128)(2,1)S(1)}, bf16[32,128,128]{2,1,0:T(8,128)(2,1)}, u32[]{:S(2)}) copy-start(bf16[32,128,128]{2,1,0:T(8,128)(2,1)} %param.9) | copy-start | bytes 3145732
  6.5 241.6 %reduce-scatter.2.cloned.1.call-start = ((), (), s32[]{:S(2)}) async-start(), calls=%async_computation.2 | async-start | bytes 9437184 | tf_op jit(solution)/shard_map/reduce_scatter | solution.py:57
  110.8 5.7 %copy-start.2 = (s32[32]{0:T(128)S(1)}, s32[32]{0:T(128)}, u32[]{:S(2)}) copy-start(s32[32]{0:T(128)} %param.14) | copy-start | bytes 388
  110.8 6.0 %copy-start.1 = (f32[32,128]{1,0:T(8,128)S(1)}, f32[32,128]{1,0:T(8,128)}, u32[]{:S(2)}) copy-start(f32[32,128]{1,0:T(8,128)} %param.10) | copy-start | bytes 49156
  149.1 0.7 copy-start.3
Sparse Core Ops, SparseCore 0:
  149.3 98.8 reduce-scatter.1
where the time goes:
time: 283 us; the launch traced here: 282 us
  waiting for transfers between devices  96.5 us (34%)
  local copies, waits for them, and re-layouts  81.7 us (29%)
  other arithmetic  55 us (19%)
  blocking collectives  24.2 us (9%)
  between operations  13.5 us (5%)
  matrix products  7.15 us (3%)
  loops' own time  3.91 us (1%)
    reduce_scatter x1, waiting for transfers between devices, radial_total(): lax.psum_scatter(partial_value, 'rad', scatter_dimension=1, tiled=True)  96.5 us
    while x441, other arithmetic  43.8 us
    dynamic_update_slice x63, local copies, waits for them, and re-layouts, build_tables(): lax.scan(advance, (start_values, second), (rec_scale[:, 1:ndeg - 1].T, re...  39.6 us
    concatenate x1, local copies, waits for them, and re-layouts, build_tables(): tables = jnp.concatenate([start_values[None], second[None], rest], axis=0)  25.2 us
    all_to_all x1, blocking collectives, body(): lax.all_to_all(summed[order], 'ell', split_axis=0, concat_axis=0, tiled=T...  24.2 us
    dot_general x1, matrix products, local_partials(): jnp.einsum('nei,eic->enc', tables, shells, preferred_element_type=jnp.flo...  7.15 us
    reshape x1, local copies, waits for them, and re-layouts, build_tables(): lax.scan(advance, (start_values, second), (rec_scale[:, 1:ndeg - 1].T, re...  5.72 us
  transfers between devices with their start and end apart: 1, of which 1 were waited for; matrix products, arithmetic and copies ran while one was open for 1% of the time, Pallas kernels for 0%

commit v1 on v0

v1 whole, which is shorter than its diff:
```python
import jax
import jax.numpy as jnp
from jax import lax
from jax.experimental import pallas as pl
from jax.experimental.pallas import tpu as pltpu
from jax.sharding import PartitionSpec as P

MESH = pl.DeviceIdType.MESH
R = 1024
NDEG = 512
C = 128
NX, NY, NC, NZ = 4, 4, 2, 8
GROUPS = NX * NY * NC
PER = GROUPS // NZ
BLOCK = R // NZ
SHARE = NDEG // NZ


def ell_index(x, y, core):
    return (lax.rem(x + 2 * NX, NX) * NY + lax.rem(y + 2 * NY, NY)) * NC + core


def split(e):
    return lax.div(e, NY * NC), lax.rem(lax.div(e, NC), NY), lax.rem(e, NC)


def owner_of(e, z, t):
    x, y, _ = split(e)
    return ell_index(x + t, y + t + lax.div(z, NC), lax.rem(z, NC))


def kernel(
    owners_ref, counts_ref, shells_ref, start_ref, scale_ref, shift_ref, damp_ref, out_ref,
    order, coef, coef_v, stage_start, stage_shells, got_start, got_shells, tables, sums,
    coef_sem, send_start, recv_start, send_shells, recv_shells, send_out, recv_out,
):
    e, z = lax.axis_index("ell"), lax.axis_index("rad")
    x, y, core = split(e)

    def device(to_e, to_z):
        return {"ell": to_e, "rad": to_z}

    barrier = pltpu.get_barrier_semaphore()
    for d in range(1, NZ):
        pl.semaphore_signal(barrier, inc=1, device_id=device(e, lax.rem(z + d, NZ)), device_id_type=MESH)
    has_self = z == core
    for t in range(PER):
        for jy in range(NY):
            for c in range(NC):
                src_e, src_z = ell_index(x - t, y - t - jy, c), jy * NC + core
                if t == 0 and jy == 0:

                    @pl.when(jnp.logical_not(jnp.logical_and(src_e == e, src_z == z)))
                    def _():
                        pl.semaphore_signal(barrier, inc=1, device_id=device(src_e, src_z), device_id_type=MESH)
                else:
                    pl.semaphore_signal(barrier, inc=1, device_id=device(src_e, src_z), device_id_type=MESH)

    words = [jnp.int32(0)] * (GROUPS // 4)
    for p in range(GROUPS):
        o = owners_ref[p]
        high, low = o >> 2, o & 3
        value = jnp.where(low == 0, p, jnp.where(low == 1, p << 8, jnp.where(low == 2, p << 16, p << 24)))
        for k in range(GROUPS // 4):
            words[k] = words[k] + jnp.where(high == k, value, 0)
    for k in range(GROUPS // 4):
        for b in range(4):
            order[4 * k + b] = (words[k] >> (8 * b)) & 31

    coef_v[...] = jnp.zeros_like(coef_v)
    stage_start[...] = jnp.zeros_like(stage_start)
    mine = [order[owner_of(e, z, t)] for t in range(PER)]
    for t in range(PER):
        for i, ref in enumerate((scale_ref, shift_ref, damp_ref)):
            coef_v[i, pl.ds(t, 1), :] = ref[pl.ds(mine[t], 1), :]
    to_scalar = pltpu.make_async_copy(coef_v, coef, coef_sem)
    to_scalar.start()

    for d in range(NZ):
        to_z = lax.rem(z + d, NZ)
        for t in range(PER):
            p = order[owner_of(e, to_z, t)]
            row = start_ref[pl.ds(p, 1), :]
            if d == 0:
                got_start[pl.ds(z * 8 + t, 1), :] = row
                got_shells[t, pl.ds(pl.multiple_of(z * BLOCK, BLOCK), BLOCK), :] = shells_ref[p]
            else:
                stage_start[d - 1, pl.ds(t, 1), :] = row
                stage_shells[d - 1, t] = shells_ref[p]

    pl.semaphore_wait(barrier, NZ - 1 + GROUPS - has_self.astype(jnp.int32))

    def start_copy(d):
        return pltpu.make_async_remote_copy(
            src_ref=stage_start.at[d - 1],
            dst_ref=got_start.at[pl.ds(pl.multiple_of(z * 8, 8), 8)],
            send_sem=send_start.at[d - 1],
            recv_sem=recv_start.at[d - 1],
            device_id=device(e, lax.rem(z + d, NZ)),
            device_id_type=MESH,
        )

    def shell_copy(t, d):
        return pltpu.make_async_remote_copy(
            src_ref=stage_shells.at[d - 1, t],
            dst_ref=got_shells.at[t, pl.ds(pl.multiple_of(z * BLOCK, BLOCK), BLOCK)],
            send_sem=send_shells.at[d - 1, t],
            recv_sem=recv_shells.at[d - 1, t],
            device_id=device(e, lax.rem(z + d, NZ)),
            device_id_type=MESH,
        )

    far_first = (4, 3, 5, 2, 6, 1, 7)
    for d in far_first:
        start_copy(d).start()
    for t in range(PER):
        for d in far_first:
            shell_copy(t, d).start()

    for d in range(1, NZ):
        start_copy(d).wait_recv()
    to_scalar.wait()

    index = lax.broadcasted_iota(jnp.int32, (NZ, BLOCK), 0) * BLOCK + lax.broadcasted_iota(jnp.int32, (NZ, BLOCK), 1)
    nodes = jnp.cos(jnp.pi * (2.0 * index.astype(jnp.float32) + 1.0) / (2.0 * R))

    def eight(block, carry):
        carry = list(carry)
        for u in range(8):
            n = block * 8 + u
            for t in range(PER):
                before, now = carry[t]
                tables[t, block, pl.ds(u, NZ, stride=8), :] = now
                after = coef[0, t, n] * (nodes + coef[1, t, n]) * now - coef[2, t, n] * before
                carry[t] = (now, after)
        return tuple(carry)

    first = tuple((jnp.zeros((NZ, BLOCK), jnp.float32), got_start[pl.ds(t, NZ, stride=8), :]) for t in range(PER))
    lax.fori_loop(0, NDEG // 8, eight, first)

    def out_copy(t, d, here=False):
        to_z = lax.rem(z + d, NZ)
        src = sums.at[t, pl.ds(pl.multiple_of(to_z * SHARE, SHARE), SHARE)]
        if here:
            return pltpu.make_async_copy(src, out_ref.at[e], recv_out.at[e])
        return pltpu.make_async_remote_copy(
            src_ref=src,
            dst_ref=out_ref.at[e],
            send_sem=send_out.at[t, d],
            recv_sem=recv_out.at[e],
            device_id=device(owner_of(e, z, t), to_z),
            device_id_type=MESH,
        )

    for t in range(PER):
        for d in range(1, NZ):
            shell_copy(t, d).wait_recv()
        live = counts_ref[mine[t]]
        rows = 128

        def dots(step, _):
            base = step * (rows // 8)
            degree = lax.broadcasted_iota(jnp.int32, (rows, BLOCK), 0) + step * rows
            keep = degree < live
            left = jnp.concatenate(
                [
                    jnp.where(keep, tables[t, pl.ds(base, rows // 8), pl.ds(s * 8, 8), :].reshape(rows, BLOCK), 0.0).astype(jnp.bfloat16)
                    for s in range(NZ)
                ],
                axis=1,
            )
            total = jnp.dot(left, got_shells[t], preferred_element_type=jnp.float32)
            sums[t, pl.ds(pl.multiple_of(step * rows, rows), rows), :] = total.astype(jnp.bfloat16)
            return 0

        lax.fori_loop(0, NDEG // rows, dots, 0)
        for d in range(NZ):
            if t == 0 and d == 0:
                pl.when(has_self)(lambda: out_copy(0, 0, here=True).start())
                pl.when(jnp.logical_not(has_self))(lambda: out_copy(0, 0).start())
            else:
                out_copy(t, d).start()

    for t in range(PER):
        for jy in range(NY):
            for c in range(NC):
                slot = ell_index(x - t, y - t - jy, c)
                pltpu.make_async_copy(out_ref.at[slot], out_ref.at[slot], recv_out.at[slot]).wait()
    for d in far_first:
        start_copy(d).wait_send()
    for t in range(PER):
        for d in far_first:
            shell_copy(t, d).wait_send()
        for d in range(NZ):
            if t == 0 and d == 0:
                pl.when(jnp.logical_not(has_self))(lambda: out_copy(0, 0).wait_send())
            else:
                out_copy(t, d).wait_send()


def body(shells, start_values, rec_scale, rec_shift, rec_damp, degree_counts, owners):
    vmem = pl.BlockSpec(memory_space=pltpu.VMEM)
    smem = pl.BlockSpec(memory_space=pltpu.SMEM)
    dma = pltpu.SemaphoreType.DMA
    arrived = pl.pallas_call(
        kernel,
        out_shape=jax.ShapeDtypeStruct((GROUPS, SHARE, C), jnp.bfloat16),
        in_specs=[smem, smem, vmem, vmem, vmem, vmem, vmem],
        out_specs=vmem,
        scratch_shapes=[
            pltpu.SMEM((GROUPS,), jnp.int32),
            pltpu.SMEM((3, 8, NDEG), jnp.float32),
            pltpu.VMEM((3, 8, NDEG), jnp.float32),
            pltpu.VMEM((NZ - 1, 8, BLOCK), jnp.float32),
            pltpu.VMEM((NZ - 1, PER, BLOCK, C), jnp.bfloat16),
            pltpu.VMEM((NZ * 8, BLOCK), jnp.float32),
            pltpu.VMEM((PER, R, C), jnp.bfloat16),
            pltpu.VMEM((PER, NDEG // 8, NZ * 8, BLOCK), jnp.float32),
            pltpu.VMEM((PER, NDEG, C), jnp.bfloat16),
            dma,
            dma((NZ - 1,)),
            dma((NZ - 1,)),
            dma((NZ - 1, PER)),
            dma((NZ - 1, PER)),
            dma((PER, NZ)),
            dma((GROUPS,)),
        ],
        compiler_params=pltpu.CompilerParams(
            collective_id=0, has_side_effects=True, vmem_limit_bytes=40 * 2**20
        ),
        name="transform",
    )(owners, degree_counts, shells, start_values, rec_scale, rec_shift, rec_damp)
    return arrived.astype(jnp.float32)


def solution(mesh):
    return jax.shard_map(
        body,
        mesh=mesh,
        in_specs=(
            P("ell", "rad", None),
            P("ell", "rad"),
            P("ell", None),
            P("ell", None),
            P("ell", None),
            P("ell"),
            P("ell"),
        ),
        out_specs=P("ell", "rad", None),
        check_vma=False,
    )
```

time: 283 us -> 58.4 us (0.21)
  waiting for transfers between devices: 96.5 us -> 0 us
  local copies, waits for them, and re-layouts: 81.7 us -> 5.77 us
  other arithmetic: 55 us -> 1.08 us
  Pallas kernels: 0 us -> 51.2 us
  blocking collectives: 24.2 us -> 0 us
  between operations: 13.5 us -> 0.02 us
  matrix products: 7.15 us -> 0 us
  loops' own time: 3.91 us -> 0 us
    reduce_scatter x1 -> x0, waiting for transfers between devices: 96.5 us -> none  [radial_total(): lax.psum_scatter(partial_value, 'rad', scatter_dimension=1, tiled=True)]
    pallas_call x0 -> x1, Pallas kernels: none -> 51.2 us  [body(): pl.pallas_call(kernel, out_shape=jax.ShapeDtypeStruct((GROUPS, SHARE, C),...]
    while x441 -> x0, other arithmetic: 43.8 us -> none
    dynamic_update_slice x63 -> x0, local copies, waits for them, and re-layouts: 39.6 us -> none  [build_tables(): lax.scan(advance, (start_values, second), (rec_scale[:, 1:ndeg - 1].T, re...]
    concatenate x1 -> x0, local copies, waits for them, and re-layouts: 25.2 us -> none  [build_tables(): tables = jnp.concatenate([start_values[None], second[None], rest], axis=0)]
    all_to_all x1 -> x0, blocking collectives: 24.2 us -> none  [body(): lax.all_to_all(summed[order], 'ell', split_axis=0, concat_axis=0, tiled=T...]
    dot_general x1 -> x0, matrix products: 7.15 us -> none  [local_partials(): jnp.einsum('nei,eic->enc', tables, shells, preferred_element_type=jnp.flo...]
    reshape x1 -> x0, local copies, waits for them, and re-layouts: 5.72 us -> none  [build_tables(): lax.scan(advance, (start_values, second), (rec_scale[:, 1:ndeg - 1].T, re...]
  transfers between devices with their start and end apart: 1 -> 0, of which waited for: 1 -> 0; matrix products, arithmetic and copies ran while one was open for 1% -> 0% of each run, Pallas kernels for 0% -> 0%
where the time goes in v1:
time: 58.4 us; the launch traced here: 58.1 us
  Pallas kernels  51.2 us (88%)
  local copies, waits for them, and re-layouts  5.77 us (10%)
  other arithmetic  1.08 us (2%)
    pallas_call x1, Pallas kernels, body(): pl.pallas_call(kernel, out_shape=jax.ShapeDtypeStruct((GROUPS, SHARE, C),...  51.2 us
    unnamed x14, local copies, waits for them, and re-layouts  5.77 us

profile of v1, /device:TPU:1, one launch (start us, length us, event | category | flops | bytes accessed | tf_op | source)
XLA Modules:
  0.0 58.1 jit_solution(3939296319921236447)
XLA Ops:
  0.0 0.0 copy-start
  0.0 1.2 %copy-done = bf16[32,128,128]{2,1,0:T(8,128)(2,1)S(1)} copy-done((bf16[32,128,128]{2,1,0:T(8,128)(2,1)S(1)}, bf16[32,128,128]{2,1,0:T(8,128)(2,1)}, u32[]{:S(2)}) %copy-start) | copy-done | bytes 1048600
  1.2 0.0 copy-start.1
  1.2 0.8 %copy-done.1 = f32[32,512]{1,0:T(8,128)S(1)} copy-done((f32[32,512]{1,0:T(8,128)S(1)}, f32[32,512]{1,0:T(8,128)}, u32[]{:S(2)}) %copy-start.1) | copy-done | bytes 65560
  2.1 0.0 copy-start.2
  2.1 0.8 %copy-done.2 = f32[32,512]{1,0:T(8,128)S(1)} copy-done((f32[32,512]{1,0:T(8,128)S(1)}, f32[32,512]{1,0:T(8,128)}, u32[]{:S(2)}) %copy-start.2) | copy-done | bytes 65560
  2.9 0.0 copy-start.3
  2.9 0.8 %copy-done.3 = f32[32,512]{1,0:T(8,128)S(1)} copy-done((f32[32,512]{1,0:T(8,128)S(1)}, f32[32,512]{1,0:T(8,128)}, u32[]{:S(2)}) %copy-start.3) | copy-done | bytes 65560
  3.7 0.0 copy-start.4
  3.7 0.7 %copy-done.4 = f32[32,128]{1,0:T(8,128)S(1)} copy-done((f32[32,128]{1,0:T(8,128)S(1)}, f32[32,128]{1,0:T(8,128)}, u32[]{:S(2)}) %copy-start.4) | copy-done | bytes 16408
  4.5 0.0 copy-start.5
  4.5 0.7 %copy-done.5 = s32[32]{0:T(128)S(1)} copy-done((s32[32]{0:T(128)S(1)}, s32[32]{0:T(128)}, u32[]{:S(2)}) %copy-start.5) | copy-done | bytes 152
  5.1 0.0 copy-start.6
  5.1 0.7 %copy-done.6 = s32[32]{0:T(128)S(1)} copy-done((s32[32]{0:T(128)S(1)}, s32[32]{0:T(128)}, u32[]{:S(2)}) %copy-start.6) | copy-done | bytes 152
  5.8 51.2 %transform.1 = bf16[32,64,128]{2,1,0:T(8,128)(2,1)S(1)} custom-call(s32[32]{0:T(128)S(1)} %copy-done.5, s32[32]{0:T(128)S(1)} %copy-done.6, bf16[32,128,128]{2,1,0:T(8,128)(2,1)S(1)} %copy-done, f32[32,128]{1,0:T(8,128)S(1)} %copy-done.4, f32[32,512]{1,0:T(8,128)S(1)} %copy-done.1, f32[32,512]{1,0:T(8,128)S(1)} %copy-done.2, f32[32,512]{1,0:T(8,128)S(1)} %copy-done.3), custom_call_target="tpu_custom_call" | custom-call | tf_op jit(solution)/shard_map/transform/pallas_call | solution.py:205
  57.0 1.1 %convert_element_type.3 = f32[32,64,128]{2,1,0:T(8,128)} convert(bf16[32,64,128]{2,1,0:T(8,128)(2,1)S(1)} %transform.1) | non-fusion elementwise | flops 262144 | bytes 1572864 | tf_op jit(solution)/shard_map/convert_element_type | solution.py:233
Async XLA Ops:
  0.0 1.2 %copy-start = (bf16[32,128,128]{2,1,0:T(8,128)(2,1)S(1)}, bf16[32,128,128]{2,1,0:T(8,128)(2,1)}, u32[]{:S(2)}) copy-start(bf16[32,128,128]{2,1,0:T(8,128)(2,1)} %shells_ref.1) | copy-start | bytes 3145732
  1.2 0.8 %copy-start.1 = (f32[32,512]{1,0:T(8,128)S(1)}, f32[32,512]{1,0:T(8,128)}, u32[]{:S(2)}) copy-start(f32[32,512]{1,0:T(8,128)} %scale_ref.1) | copy-start | bytes 196612
  2.1 0.8 %copy-start.2 = (f32[32,512]{1,0:T(8,128)S(1)}, f32[32,512]{1,0:T(8,128)}, u32[]{:S(2)}) copy-start(f32[32,512]{1,0:T(8,128)} %shift_ref.1) | copy-start | bytes 196612
  2.9 0.8 %copy-start.3 = (f32[32,512]{1,0:T(8,128)S(1)}, f32[32,512]{1,0:T(8,128)}, u32[]{:S(2)}) copy-start(f32[32,512]{1,0:T(8,128)} %damp_ref.1) | copy-start | bytes 196612
  3.7 0.7 %copy-start.4 = (f32[32,128]{1,0:T(8,128)S(1)}, f32[32,128]{1,0:T(8,128)}, u32[]{:S(2)}) copy-start(f32[32,128]{1,0:T(8,128)} %start_ref.1) | copy-start | bytes 49156
  4.5 0.7 %copy-start.5 = (s32[32]{0:T(128)S(1)}, s32[32]{0:T(128)}, u32[]{:S(2)}) copy-start(s32[32]{0:T(128)} %owners_ref.1) | copy-start | bytes 388
  5.1 0.7 %copy-start.6 = (s32[32]{0:T(128)S(1)}, s32[32]{0:T(128)}, u32[]{:S(2)}) copy-start(s32[32]{0:T(128)} %counts_ref.1) | copy-start | bytes 388

commit v2 on v1

--- a/solution.py
+++ b/solution.py
@@ -30,7 +30,8 @@
 
 
 def kernel(
-    owners_ref, counts_ref, shells_ref, start_ref, scale_ref, shift_ref, damp_ref, out_ref,
+    owners_hbm, counts_hbm, shells_hbm, start_hbm, scale_hbm, shift_hbm, damp_hbm, out_ref,
+    owners_ref, counts_ref, shells_ref, start_ref, scale_ref, shift_ref, damp_ref, load_sem,
     order, coef, coef_v, stage_start, stage_shells, got_start, got_shells, tables, sums,
     coef_sem, send_start, recv_start, send_shells, recv_shells, send_out, recv_out,
 ):
@@ -40,6 +41,30 @@
     def device(to_e, to_z):
         return {"ell": to_e, "rad": to_z}
 
+    parts = 4
+    loads = [
+        pltpu.make_async_copy(src, dst, load_sem.at[i])
+        for i, (src, dst) in enumerate(
+            (
+                (owners_hbm, owners_ref),
+                (start_hbm, start_ref),
+                (counts_hbm, counts_ref),
+                (scale_hbm, scale_ref),
+                (shift_hbm, shift_ref),
+                (damp_hbm, damp_ref),
+            )
+        )
+    ]
+    part = GROUPS // parts
+    loads += [
+        pltpu.make_async_copy(
+            shells_hbm.at[pl.ds(i * part, part)], shells_ref.at[pl.ds(i * part, part)], load_sem.at[6 + i]
+        )
+        for i in range(parts)
+    ]
+    for load in loads:
+        load.start()
+
     barrier = pltpu.get_barrier_semaphore()
     for d in range(1, NZ):
         pl.semaphore_signal(barrier, inc=1, device_id=device(e, lax.rem(z + d, NZ)), device_id_type=MESH)
@@ -56,6 +81,7 @@
                 else:
                     pl.semaphore_signal(barrier, inc=1, device_id=device(src_e, src_z), device_id_type=MESH)
 
+    loads[0].wait()
     words = [jnp.int32(0)] * (GROUPS // 4)
     for p in range(GROUPS):
         o = owners_ref[p]
@@ -67,6 +93,8 @@
         for b in range(4):
             order[4 * k + b] = (words[k] >> (8 * b)) & 31
 
+    for load in loads[1:6]:
+        load.wait()
     coef_v[...] = jnp.zeros_like(coef_v)
     stage_start[...] = jnp.zeros_like(stage_start)
     mine = [order[owner_of(e, z, t)] for t in range(PER)]
@@ -76,6 +104,8 @@
     to_scalar = pltpu.make_async_copy(coef_v, coef, coef_sem)
     to_scalar.start()
 
+    for load in loads[6:]:
+        load.wait()
     for d in range(NZ):
         to_z = lax.rem(z + d, NZ)
         for t in range(PER):
@@ -199,15 +229,22 @@
 
 
 def body(shells, start_values, rec_scale, rec_shift, rec_damp, degree_counts, owners):
-    vmem = pl.BlockSpec(memory_space=pltpu.VMEM)
-    smem = pl.BlockSpec(memory_space=pltpu.SMEM)
+    hbm = pl.BlockSpec(memory_space=pltpu.HBM)
     dma = pltpu.SemaphoreType.DMA
     arrived = pl.pallas_call(
         kernel,
         out_shape=jax.ShapeDtypeStruct((GROUPS, SHARE, C), jnp.bfloat16),
-        in_specs=[smem, smem, vmem, vmem, vmem, vmem, vmem],
-        out_specs=vmem,
+        in_specs=[hbm] * 7,
+        out_specs=hbm,
         scratch_shapes=[
+            pltpu.SMEM((GROUPS,), jnp.int32),
+            pltpu.SMEM((GROUPS,), jnp.int32),
+            pltpu.VMEM((GROUPS, BLOCK, C), jnp.bfloat16),
+            pltpu.VMEM((GROUPS, BLOCK), jnp.float32),
+            pltpu.VMEM((GROUPS, NDEG), jnp.float32),
+            pltpu.VMEM((GROUPS, NDEG), jnp.float32),
+            pltpu.VMEM((GROUPS, NDEG), jnp.float32),
+            dma((10,)),
             pltpu.SMEM((GROUPS,), jnp.int32),
             pltpu.SMEM((3, 8, NDEG), jnp.float32),
             pltpu.VMEM((3, 8, NDEG), jnp.float32),
@@ -226,7 +263,7 @@
             dma((GROUPS,)),
         ],
         compiler_params=pltpu.CompilerParams(
-            collective_id=0, has_side_effects=True, vmem_limit_bytes=40 * 2**20
+            collective_id=0, has_side_effects=True, vmem_limit_bytes=62 * 2**20 - 2**18
         ),
         name="transform",
     )(owners, degree_counts, shells, start_values, rec_scale, rec_shift, rec_damp)

time: 58.4 us -> 53.2 us (0.911)
  local copies, waits for them, and re-layouts: 5.77 us -> 0 us
  other arithmetic: 1.08 us -> 2.13 us
    unnamed x14 -> x0, local copies, waits for them, and re-layouts: 5.77 us -> none
    convert_element_type x1, other arithmetic: 1.08 us -> 2.13 us  [body(): return arrived.astype(jnp.float32)]
where the time goes in v2:
time: 53.2 us; the launch traced here: 53 us
  Pallas kernels  50.9 us (96%)
  other arithmetic  2.13 us (4%)
    pallas_call x1, Pallas kernels, body(): pl.pallas_call(kernel, out_shape=jax.ShapeDtypeStruct((GROUPS, SHARE, C),...  50.9 us
    convert_element_type x1, other arithmetic, body(): return arrived.astype(jnp.float32)  2.13 us

profile of v2, /device:TPU:1, one launch (start us, length us, event | category | flops | bytes accessed | tf_op | source)
XLA Modules:
  0.0 53.0 jit_solution(12195069962528495289)
XLA Ops:
  0.0 50.9 %transform.1 = bf16[32,64,128]{2,1,0:T(8,128)(2,1)} custom-call(s32[32]{0:T(128)} %owners_hbm.1, s32[32]{0:T(128)} %counts_hbm.1, bf16[32,128,128]{2,1,0:T(8,128)(2,1)} %shells_hbm.1, f32[32,128]{1,0:T(8,128)} %start_hbm.1, f32[32,512]{1,0:T(8,128)} %scale_hbm.1, f32[32,512]{1,0:T(8,128)} %shift_hbm.1, f32[32,512]{1,0:T(8,128)} %damp_hbm.1), custom_call_target="tpu_custom_call" | custom-call | tf_op jit(solution)/shard_map/transform/pallas_call | solution.py:234
  50.9 2.1 %convert_element_type.3 = f32[32,64,128]{2,1,0:T(8,128)} convert(bf16[32,64,128]{2,1,0:T(8,128)(2,1)} %transform.1) | non-fusion elementwise | flops 262144 | bytes 1572864 | tf_op jit(solution)/shard_map/convert_element_type | solution.py:270

commit v3 on v2

--- a/solution.py
+++ b/solution.py
@@ -25,18 +25,22 @@
 
 
 def owner_of(e, z, t):
-    x, y, _ = split(e)
-    return ell_index(x + t, y + t + lax.div(z, NC), lax.rem(z, NC))
+    x, y, core = split(e)
+    return ell_index(x + t, y + t + lax.div(z, NC), lax.rem(core + z, NC))
+
+
+def group_of(o, z, t):
+    x, y, core = split(o)
+    return ell_index(x - t, y - t - lax.div(z, NC), lax.rem(core + z, NC))
 
 
 def kernel(
     owners_hbm, counts_hbm, shells_hbm, start_hbm, scale_hbm, shift_hbm, damp_hbm, out_ref,
     owners_ref, counts_ref, shells_ref, start_ref, scale_ref, shift_ref, damp_ref, load_sem,
-    order, coef, coef_v, stage_start, stage_shells, got_start, got_shells, tables, sums,
-    coef_sem, send_start, recv_start, send_shells, recv_shells, send_out, recv_out,
+    order, coef, coef_v, stage_start, stage_shells, got_start, got_shells, tables, rounded, sums, hopped,
+    coef_sem, send_start, recv_start, send_shells, recv_shells, send_hop, recv_hop, send_out, recv_out,
 ):
     e, z = lax.axis_index("ell"), lax.axis_index("rad")
-    x, y, core = split(e)
 
     def device(to_e, to_z):
         return {"ell": to_e, "rad": to_z}
@@ -68,18 +72,16 @@
     barrier = pltpu.get_barrier_semaphore()
     for d in range(1, NZ):
         pl.semaphore_signal(barrier, inc=1, device_id=device(e, lax.rem(z + d, NZ)), device_id_type=MESH)
-    has_self = z == core
-    for t in range(PER):
-        for jy in range(NY):
-            for c in range(NC):
-                src_e, src_z = ell_index(x - t, y - t - jy, c), jy * NC + core
-                if t == 0 and jy == 0:
-
-                    @pl.when(jnp.logical_not(jnp.logical_and(src_e == e, src_z == z)))
-                    def _():
-                        pl.semaphore_signal(barrier, inc=1, device_id=device(src_e, src_z), device_id_type=MESH)
-                else:
-                    pl.semaphore_signal(barrier, inc=1, device_id=device(src_e, src_z), device_id_type=MESH)
+    stays = z == 0
+    for t in range(PER):
+
+        def greet(t=t):
+            pl.semaphore_signal(barrier, inc=1, device_id=device(group_of(e, z, t), z), device_id_type=MESH)
+
+        if t == 0:
+            pl.when(jnp.logical_not(stays))(greet)
+        else:
+            greet()
 
     loads[0].wait()
     words = [jnp.int32(0)] * (GROUPS // 4)
@@ -93,33 +95,6 @@
         for b in range(4):
             order[4 * k + b] = (words[k] >> (8 * b)) & 31
 
-    for load in loads[1:6]:
-        load.wait()
-    coef_v[...] = jnp.zeros_like(coef_v)
-    stage_start[...] = jnp.zeros_like(stage_start)
-    mine = [order[owner_of(e, z, t)] for t in range(PER)]
-    for t in range(PER):
-        for i, ref in enumerate((scale_ref, shift_ref, damp_ref)):
-            coef_v[i, pl.ds(t, 1), :] = ref[pl.ds(mine[t], 1), :]
-    to_scalar = pltpu.make_async_copy(coef_v, coef, coef_sem)
-    to_scalar.start()
-
-    for load in loads[6:]:
-        load.wait()
-    for d in range(NZ):
-        to_z = lax.rem(z + d, NZ)
-        for t in range(PER):
-            p = order[owner_of(e, to_z, t)]
-            row = start_ref[pl.ds(p, 1), :]
-            if d == 0:
-                got_start[pl.ds(z * 8 + t, 1), :] = row
-                got_shells[t, pl.ds(pl.multiple_of(z * BLOCK, BLOCK), BLOCK), :] = shells_ref[p]
-            else:
-                stage_start[d - 1, pl.ds(t, 1), :] = row
-                stage_shells[d - 1, t] = shells_ref[p]
-
-    pl.semaphore_wait(barrier, NZ - 1 + GROUPS - has_self.astype(jnp.int32))
-
     def start_copy(d):
         return pltpu.make_async_remote_copy(
             src_ref=stage_start.at[d - 1],
@@ -141,11 +116,38 @@
         )
 
     far_first = (4, 3, 5, 2, 6, 1, 7)
+    loads[1].wait()
+    stage_start[...] = jnp.zeros_like(stage_start)
+    to = [[order[owner_of(e, lax.rem(z + d, NZ), t)] for t in range(PER)] for d in range(NZ)]
+    for d in range(1, NZ):
+        for t in range(PER):
+            stage_start[d - 1, pl.ds(t, 1), :] = start_ref[pl.ds(to[d][t], 1), :]
+    for load in loads[6:]:
+        load.wait()
     for d in far_first:
+        stage_shells[d - 1, 0] = shells_ref[to[d][0]]
+    pl.semaphore_wait(barrier, NZ - 1 + PER - stays.astype(jnp.int32))
+    for d in far_first:
+        shell_copy(0, d).start()
         start_copy(d).start()
-    for t in range(PER):
+    for t in range(1, PER):
         for d in far_first:
+            stage_shells[d - 1, t] = shells_ref[to[d][t]]
             shell_copy(t, d).start()
+
+    mine = to[0]
+    for t in range(PER):
+        got_start[pl.ds(z * 8 + t, 1), :] = start_ref[pl.ds(mine[t], 1), :]
+        got_shells[t, pl.ds(pl.multiple_of(z * BLOCK, BLOCK), BLOCK), :] = shells_ref[mine[t]]
+
+    for load in loads[2:6]:
+        load.wait()
+    coef_v[...] = jnp.zeros_like(coef_v)
+    for t in range(PER):
+        for i, ref in enumerate((scale_ref, shift_ref, damp_ref)):
+            coef_v[i, pl.ds(t, 1), :] = ref[pl.ds(mine[t], 1), :]
+    to_scalar = pltpu.make_async_copy(coef_v, coef, coef_sem)
+    to_scalar.start()
 
     for d in range(1, NZ):
         start_copy(d).wait_recv()
@@ -168,64 +170,80 @@
     first = tuple((jnp.zeros((NZ, BLOCK), jnp.float32), got_start[pl.ds(t, NZ, stride=8), :]) for t in range(PER))
     lax.fori_loop(0, NDEG // 8, eight, first)
 
-    def out_copy(t, d, here=False):
+    def hop_copy(t):
+        return pltpu.make_async_remote_copy(
+            src_ref=sums.at[t],
+            dst_ref=hopped.at[t],
+            send_sem=send_hop.at[t],
+            recv_sem=recv_hop.at[t],
+            device_id=device(owner_of(e, z, t), z),
+            device_id_type=MESH,
+        )
+
+    def hop_here(t):
+        return pltpu.make_async_copy(sums.at[t], hopped.at[t], recv_hop.at[t])
+
+    def out_copy(t, d):
         to_z = lax.rem(z + d, NZ)
-        src = sums.at[t, pl.ds(pl.multiple_of(to_z * SHARE, SHARE), SHARE)]
-        if here:
-            return pltpu.make_async_copy(src, out_ref.at[e], recv_out.at[e])
+        slot = group_of(e, z, t)
+        src = hopped.at[t, pl.ds(pl.multiple_of(to_z * SHARE, SHARE), SHARE)]
+        if d == 0:
+            return pltpu.make_async_copy(src, out_ref.at[slot], recv_out.at[slot])
         return pltpu.make_async_remote_copy(
             src_ref=src,
-            dst_ref=out_ref.at[e],
-            send_sem=send_out.at[t, d],
-            recv_sem=recv_out.at[e],
-            device_id=device(owner_of(e, z, t), to_z),
+            dst_ref=out_ref.at[slot],
+            send_sem=send_out.at[t, d - 1],
+            recv_sem=recv_out.at[slot],
+            device_id=device(e, to_z),
             device_id_type=MESH,
         )
+
+    def forward(t):
+        hop_here(t).wait()
+        for d in (*far_first, 0):
+            out_copy(t, d).start()
+
+    rows = 128
+    for t in range(PER):
+        live = counts_ref[mine[t]]
+
+        def round_rows(step, _):
+            degree = lax.broadcasted_iota(jnp.int32, (rows, BLOCK), 0) + step * rows
+            for s in range(NZ):
+                tall = tables[t, pl.ds(step * (rows // 8), rows // 8), pl.ds(s * 8, 8), :].reshape(rows, BLOCK)
+                rounded[t, pl.ds(pl.multiple_of(step * rows, rows), rows), pl.ds(s * BLOCK, BLOCK)] = jnp.where(
+                    degree < live, tall, 0.0
+                ).astype(jnp.bfloat16)
+            return 0
+
+        lax.fori_loop(0, NDEG // rows, round_rows, 0)
 
     for t in range(PER):
         for d in range(1, NZ):
             shell_copy(t, d).wait_recv()
-        live = counts_ref[mine[t]]
-        rows = 128
-
-        def dots(step, _):
-            base = step * (rows // 8)
-            degree = lax.broadcasted_iota(jnp.int32, (rows, BLOCK), 0) + step * rows
-            keep = degree < live
-            left = jnp.concatenate(
-                [
-                    jnp.where(keep, tables[t, pl.ds(base, rows // 8), pl.ds(s * 8, 8), :].reshape(rows, BLOCK), 0.0).astype(jnp.bfloat16)
-                    for s in range(NZ)
-                ],
-                axis=1,
-            )
-            total = jnp.dot(left, got_shells[t], preferred_element_type=jnp.float32)
-            sums[t, pl.ds(pl.multiple_of(step * rows, rows), rows), :] = total.astype(jnp.bfloat16)
-            return 0
-
-        lax.fori_loop(0, NDEG // rows, dots, 0)
-        for d in range(NZ):
-            if t == 0 and d == 0:
-                pl.when(has_self)(lambda: out_copy(0, 0, here=True).start())
-                pl.when(jnp.logical_not(has_self))(lambda: out_copy(0, 0).start())
-            else:
-                out_copy(t, d).start()
-
-    for t in range(PER):
-        for jy in range(NY):
-            for c in range(NC):
-                slot = ell_index(x - t, y - t - jy, c)
-                pltpu.make_async_copy(out_ref.at[slot], out_ref.at[slot], recv_out.at[slot]).wait()
+        total = jnp.dot(rounded[t], got_shells[t], preferred_element_type=jnp.float32)
+        sums[t] = total.astype(jnp.bfloat16)
+        if t == 0:
+            pl.when(stays)(lambda: hop_here(0).start())
+            pl.when(jnp.logical_not(stays))(lambda: hop_copy(0).start())
+        else:
+            hop_copy(t).start()
+            forward(t - 1)
+    forward(PER - 1)
+
+    for j in range(NZ):
+        for t in range(PER):
+            slot = group_of(e, j, t)
+            pltpu.make_async_copy(out_ref.at[slot], out_ref.at[slot], recv_out.at[slot]).wait()
+    pl.when(jnp.logical_not(stays))(lambda: hop_copy(0).wait_send())
+    for t in range(1, PER):
+        hop_copy(t).wait_send()
     for d in far_first:
         start_copy(d).wait_send()
     for t in range(PER):
         for d in far_first:
             shell_copy(t, d).wait_send()
-        for d in range(NZ):
-            if t == 0 and d == 0:
-                pl.when(jnp.logical_not(has_self))(lambda: out_copy(0, 0).wait_send())
-            else:
-                out_copy(t, d).wait_send()
+            out_copy(t, d).wait_send()
 
 
 def body(shells, start_values, rec_scale, rec_shift, rec_damp, degree_counts, owners):
@@ -253,13 +271,17 @@
             pltpu.VMEM((NZ * 8, BLOCK), jnp.float32),
             pltpu.VMEM((PER, R, C), jnp.bfloat16),
             pltpu.VMEM((PER, NDEG // 8, NZ * 8, BLOCK), jnp.float32),
+            pltpu.VMEM((PER, NDEG, R), jnp.bfloat16),
+            pltpu.VMEM((PER, NDEG, C), jnp.bfloat16),
             pltpu.VMEM((PER, NDEG, C), jnp.bfloat16),
             dma,
             dma((NZ - 1,)),
             dma((NZ - 1,)),
             dma((NZ - 1, PER)),
             dma((NZ - 1, PER)),
-            dma((PER, NZ)),
+            dma((PER,)),
+            dma((PER,)),
+            dma((PER, NZ - 1)),
             dma((GROUPS,)),
         ],
         compiler_params=pltpu.CompilerParams(

time: 53.2 us -> 51.2 us (0.962)
  Pallas kernels: 50.9 us -> 48.9 us
    pallas_call x1, Pallas kernels: 50.9 us -> 48.9 us  [body(): pl.pallas_call(kernel, out_shape=jax.ShapeDtypeStruct((GROUPS, SHARE, C),...]
where the time goes in v3:
time: 51.2 us; the launch traced here: 51 us
  Pallas kernels  48.9 us (96%)
  other arithmetic  2.13 us (4%)
    pallas_call x1, Pallas kernels, body(): pl.pallas_call(kernel, out_shape=jax.ShapeDtypeStruct((GROUPS, SHARE, C),...  48.9 us
    convert_element_type x1, other arithmetic, body(): return arrived.astype(jnp.float32)  2.13 us

profile of v3, /device:TPU:1, one launch (start us, length us, event | category | flops | bytes accessed | tf_op | source)
XLA Modules:
  0.0 51.0 jit_solution(6615935439334328421)
XLA Ops:
  0.0 48.9 %transform.1 = bf16[32,64,128]{2,1,0:T(8,128)(2,1)} custom-call(s32[32]{0:T(128)} %owners_hbm.1, s32[32]{0:T(128)} %counts_hbm.1, bf16[32,128,128]{2,1,0:T(8,128)(2,1)} %shells_hbm.1, f32[32,128]{1,0:T(8,128)} %start_hbm.1, f32[32,512]{1,0:T(8,128)} %scale_hbm.1, f32[32,512]{1,0:T(8,128)} %shift_hbm.1, f32[32,512]{1,0:T(8,128)} %damp_hbm.1), custom_call_target="tpu_custom_call" | custom-call | tf_op jit(solution)/shard_map/transform/pallas_call | solution.py:252
  48.9 2.1 %convert_element_type.3 = f32[32,64,128]{2,1,0:T(8,128)} convert(bf16[32,64,128]{2,1,0:T(8,128)(2,1)} %transform.1) | non-fusion elementwise | flops 262144 | bytes 1572864 | tf_op jit(solution)/shard_map/convert_element_type | solution.py:292

commit v4 on v3

--- a/solution.py
+++ b/solution.py
@@ -14,6 +14,8 @@
 PER = GROUPS // NZ
 BLOCK = R // NZ
 SHARE = NDEG // NZ
+STEPS = (2, 3, 1, 0)
+HOME = 3
 
 
 def ell_index(x, y, core):
@@ -26,12 +28,15 @@
 
 def owner_of(e, z, t):
     x, y, core = split(e)
-    return ell_index(x + t, y + t + lax.div(z, NC), lax.rem(core + z, NC))
+    way = 1 - 2 * core
+    return ell_index(x + way * STEPS[t], y + way * (STEPS[t] + lax.div(z, NC)), lax.rem(core + z, NC))
 
 
 def group_of(o, z, t):
     x, y, core = split(o)
-    return ell_index(x - t, y - t - lax.div(z, NC), lax.rem(core + z, NC))
+    core = lax.rem(core + z, NC)
+    way = 1 - 2 * core
+    return ell_index(x - way * STEPS[t], y - way * (STEPS[t] + lax.div(z, NC)), core)
 
 
 def kernel(
@@ -78,7 +83,7 @@
         def greet(t=t):
             pl.semaphore_signal(barrier, inc=1, device_id=device(group_of(e, z, t), z), device_id_type=MESH)
 
-        if t == 0:
+        if t == HOME:
             pl.when(jnp.logical_not(stays))(greet)
         else:
             greet()
@@ -127,13 +132,18 @@
     for d in far_first:
         stage_shells[d - 1, 0] = shells_ref[to[d][0]]
     pl.semaphore_wait(barrier, NZ - 1 + PER - stays.astype(jnp.int32))
+    def send(t):
+        for d in far_first:
+            shell_copy(t, d).start()
+
     for d in far_first:
-        shell_copy(0, d).start()
         start_copy(d).start()
+    send(0)
     for t in range(1, PER):
         for d in far_first:
             stage_shells[d - 1, t] = shells_ref[to[d][t]]
-            shell_copy(t, d).start()
+        if t == 1:
+            send(1)
 
     mine = to[0]
     for t in range(PER):
@@ -183,25 +193,27 @@
     def hop_here(t):
         return pltpu.make_async_copy(sums.at[t], hopped.at[t], recv_hop.at[t])
 
-    def out_copy(t, d):
-        to_z = lax.rem(z + d, NZ)
+    def out_copy(t, k, here=False):
         slot = group_of(e, z, t)
-        src = hopped.at[t, pl.ds(pl.multiple_of(to_z * SHARE, SHARE), SHARE)]
-        if d == 0:
+        src = hopped.at[t, pl.ds(k * SHARE, SHARE)]
+        if here:
             return pltpu.make_async_copy(src, out_ref.at[slot], recv_out.at[slot])
         return pltpu.make_async_remote_copy(
             src_ref=src,
             dst_ref=out_ref.at[slot],
-            send_sem=send_out.at[t, d - 1],
+            send_sem=send_out.at[t, k],
             recv_sem=recv_out.at[slot],
-            device_id=device(e, to_z),
+            device_id=device(e, k),
             device_id_type=MESH,
         )
 
-    def forward(t):
+    def forward(t, planes):
+        for k in planes:
+            pl.when(z == k)(lambda k=k: out_copy(t, k, here=True).start())
+            pl.when(z != k)(lambda k=k: out_copy(t, k).start())
+
+    def hop_in(t):
         hop_here(t).wait()
-        for d in (*far_first, 0):
-            out_copy(t, d).start()
 
     rows = 128
     for t in range(PER):
@@ -218,32 +230,47 @@
 
         lax.fori_loop(0, NDEG // rows, round_rows, 0)
 
-    for t in range(PER):
+    def work(t):
         for d in range(1, NZ):
             shell_copy(t, d).wait_recv()
         total = jnp.dot(rounded[t], got_shells[t], preferred_element_type=jnp.float32)
         sums[t] = total.astype(jnp.bfloat16)
-        if t == 0:
-            pl.when(stays)(lambda: hop_here(0).start())
-            pl.when(jnp.logical_not(stays))(lambda: hop_copy(0).start())
+        if t == HOME:
+            pl.when(stays)(lambda: hop_here(HOME).start())
+            pl.when(jnp.logical_not(stays))(lambda: hop_copy(HOME).start())
         else:
             hop_copy(t).start()
-            forward(t - 1)
-    forward(PER - 1)
+
+    send(2)
+    work(0)
+    work(1)
+    send(3)
+    hop_in(0)
+    forward(0, (0, 1, 2, 3, 7, 6, 4, 5))
+    work(2)
+    hop_in(1)
+    forward(1, (0, 1, 2, 3, 7, 6, 4, 5))
+    work(3)
+    hop_in(2)
+    forward(2, (0, 1, 2, 3, 7, 6, 4, 5))
+    hop_in(3)
+    forward(3, (0, 1, 2, 3, 7, 6, 4, 5))
 
     for j in range(NZ):
         for t in range(PER):
             slot = group_of(e, j, t)
             pltpu.make_async_copy(out_ref.at[slot], out_ref.at[slot], recv_out.at[slot]).wait()
-    pl.when(jnp.logical_not(stays))(lambda: hop_copy(0).wait_send())
-    for t in range(1, PER):
-        hop_copy(t).wait_send()
+    pl.when(jnp.logical_not(stays))(lambda: hop_copy(HOME).wait_send())
+    for t in range(PER):
+        if t != HOME:
+            hop_copy(t).wait_send()
     for d in far_first:
         start_copy(d).wait_send()
     for t in range(PER):
         for d in far_first:
             shell_copy(t, d).wait_send()
-            out_copy(t, d).wait_send()
+        for k in range(NZ):
+            pl.when(z != k)(lambda t=t, k=k: out_copy(t, k).wait_send())
 
 
 def body(shells, start_values, rec_scale, rec_shift, rec_damp, degree_counts, owners):
@@ -251,9 +278,9 @@
     dma = pltpu.SemaphoreType.DMA
     arrived = pl.pallas_call(
         kernel,
-        out_shape=jax.ShapeDtypeStruct((GROUPS, SHARE, C), jnp.bfloat16),
+        out_shape=pltpu.VMEM((GROUPS, SHARE, C), jnp.bfloat16),
         in_specs=[hbm] * 7,
-        out_specs=hbm,
+        out_specs=pl.BlockSpec(memory_space=pltpu.VMEM),
         scratch_shapes=[
             pltpu.SMEM((GROUPS,), jnp.int32),
             pltpu.SMEM((GROUPS,), jnp.int32),
@@ -281,14 +308,19 @@
             dma((NZ - 1, PER)),
             dma((PER,)),
             dma((PER,)),
-            dma((PER, NZ - 1)),
+            dma((PER, NZ)),
             dma((GROUPS,)),
         ],
         compiler_params=pltpu.CompilerParams(
-            collective_id=0, has_side_effects=True, vmem_limit_bytes=62 * 2**20 - 2**18
+            collective_id=0, has_side_effects=True, vmem_limit_bytes=40 * 2**20
         ),
         name="transform",
-    )(owners, degree_counts, shells, start_values, rec_scale, rec_shift, rec_damp)
+    )(
+        *(
+            pltpu.with_memory_space_constraint(a, pltpu.HBM)
+            for a in (owners, degree_counts, shells, start_values, rec_scale, rec_shift, rec_damp)
+        )
+    )
     return arrived.astype(jnp.float32)
 
 

time: 51.2 us -> 48.6 us (0.949)
  Pallas kernels: 48.9 us -> 47.5 us
  other arithmetic: 2.13 us -> 1.09 us
    pallas_call x1, Pallas kernels: 48.9 us -> 47.5 us  [body(): pl.pallas_call(kernel, out_shape=pltpu.VMEM((GROUPS, SHARE, C), jnp.bfloa...]
    convert_element_type x1, other arithmetic: 2.13 us -> 1.09 us  [body(): return arrived.astype(jnp.float32)]
where the time goes in v4:
time: 48.6 us
  Pallas kernels  47.5 us (98%)
  other arithmetic  1.09 us (2%)
    pallas_call x1, Pallas kernels, body(): pl.pallas_call(kernel, out_shape=pltpu.VMEM((GROUPS, SHARE, C), jnp.bfloa...  47.5 us
    convert_element_type x1, other arithmetic, body(): return arrived.astype(jnp.float32)  1.09 us

profile of v4, /device:TPU:1, one launch (start us, length us, event | category | flops | bytes accessed | tf_op | source)
XLA Modules:
  0.0 48.6 jit_solution(13322679774053986426)
XLA Ops:
  0.0 47.5 %transform.1 = bf16[32,64,128]{2,1,0:T(8,128)(2,1)S(1)} custom-call(s32[32]{0:T(128)} %owners_hbm.1, s32[32]{0:T(128)} %counts_hbm.1, bf16[32,128,128]{2,1,0:T(8,128)(2,1)} %shells_hbm.1, f32[32,128]{1,0:T(8,128)} %start_hbm.1, f32[32,512]{1,0:T(8,128)} %scale_hbm.1, f32[32,512]{1,0:T(8,128)} %shift_hbm.1, f32[32,512]{1,0:T(8,128)} %damp_hbm.1), custom_call_target="tpu_custom_call" | custom-call | tf_op jit(solution)/shard_map/transform/pallas_call | solution.py:279
  47.5 1.1 %convert_element_type.3 = f32[32,64,128]{2,1,0:T(8,128)} convert(bf16[32,64,128]{2,1,0:T(8,128)(2,1)S(1)} %transform.1) | non-fusion elementwise | flops 262144 | bytes 1572864 | tf_op jit(solution)/shard_map/convert_element_type | solution.py:324

commit v5 on v4

--- a/solution.py
+++ b/solution.py
@@ -100,12 +100,15 @@
         for b in range(4):
             order[4 * k + b] = (words[k] >> (8 * b)) & 31
 
+    def arrive(ref, sem):
+        pltpu.make_async_copy(ref, ref, sem).wait()
+
     def start_copy(d):
         return pltpu.make_async_remote_copy(
             src_ref=stage_start.at[d - 1],
             dst_ref=got_start.at[pl.ds(pl.multiple_of(z * 8, 8), 8)],
-            send_sem=send_start.at[d - 1],
-            recv_sem=recv_start.at[d - 1],
+            send_sem=send_start,
+            recv_sem=recv_start,
             device_id=device(e, lax.rem(z + d, NZ)),
             device_id_type=MESH,
         )
@@ -114,8 +117,8 @@
         return pltpu.make_async_remote_copy(
             src_ref=stage_shells.at[d - 1, t],
             dst_ref=got_shells.at[t, pl.ds(pl.multiple_of(z * BLOCK, BLOCK), BLOCK)],
-            send_sem=send_shells.at[d - 1, t],
-            recv_sem=recv_shells.at[d - 1, t],
+            send_sem=send_shells,
+            recv_sem=recv_shells.at[t],
             device_id=device(e, lax.rem(z + d, NZ)),
             device_id_type=MESH,
         )
@@ -142,8 +145,8 @@
     for t in range(1, PER):
         for d in far_first:
             stage_shells[d - 1, t] = shells_ref[to[d][t]]
-        if t == 1:
-            send(1)
+        if t <= 2:
+            send(t)
 
     mine = to[0]
     for t in range(PER):
@@ -159,8 +162,7 @@
     to_scalar = pltpu.make_async_copy(coef_v, coef, coef_sem)
     to_scalar.start()
 
-    for d in range(1, NZ):
-        start_copy(d).wait_recv()
+    arrive(got_start.at[pl.ds(0, (NZ - 1) * 8)], recv_start)
     to_scalar.wait()
 
     index = lax.broadcasted_iota(jnp.int32, (NZ, BLOCK), 0) * BLOCK + lax.broadcasted_iota(jnp.int32, (NZ, BLOCK), 1)
@@ -184,7 +186,7 @@
         return pltpu.make_async_remote_copy(
             src_ref=sums.at[t],
             dst_ref=hopped.at[t],
-            send_sem=send_hop.at[t],
+            send_sem=send_hop,
             recv_sem=recv_hop.at[t],
             device_id=device(owner_of(e, z, t), z),
             device_id_type=MESH,
@@ -197,12 +199,12 @@
         slot = group_of(e, z, t)
         src = hopped.at[t, pl.ds(k * SHARE, SHARE)]
         if here:
-            return pltpu.make_async_copy(src, out_ref.at[slot], recv_out.at[slot])
+            return pltpu.make_async_copy(src, out_ref.at[slot], recv_out)
         return pltpu.make_async_remote_copy(
             src_ref=src,
             dst_ref=out_ref.at[slot],
-            send_sem=send_out.at[t, k],
-            recv_sem=recv_out.at[slot],
+            send_sem=send_out,
+            recv_sem=recv_out,
             device_id=device(e, k),
             device_id_type=MESH,
         )
@@ -231,8 +233,7 @@
         lax.fori_loop(0, NDEG // rows, round_rows, 0)
 
     def work(t):
-        for d in range(1, NZ):
-            shell_copy(t, d).wait_recv()
+        arrive(got_shells.at[t, pl.ds(0, (NZ - 1) * BLOCK)], recv_shells.at[t])
         total = jnp.dot(rounded[t], got_shells[t], preferred_element_type=jnp.float32)
         sums[t] = total.astype(jnp.bfloat16)
         if t == HOME:
@@ -241,10 +242,9 @@
         else:
             hop_copy(t).start()
 
-    send(2)
     work(0)
+    send(3)
     work(1)
-    send(3)
     hop_in(0)
     forward(0, (0, 1, 2, 3, 7, 6, 4, 5))
     work(2)
@@ -255,22 +255,12 @@
     forward(2, (0, 1, 2, 3, 7, 6, 4, 5))
     hop_in(3)
     forward(3, (0, 1, 2, 3, 7, 6, 4, 5))
-
-    for j in range(NZ):
-        for t in range(PER):
-            slot = group_of(e, j, t)
-            pltpu.make_async_copy(out_ref.at[slot], out_ref.at[slot], recv_out.at[slot]).wait()
-    pl.when(jnp.logical_not(stays))(lambda: hop_copy(HOME).wait_send())
-    for t in range(PER):
-        if t != HOME:
-            hop_copy(t).wait_send()
-    for d in far_first:
-        start_copy(d).wait_send()
-    for t in range(PER):
-        for d in far_first:
-            shell_copy(t, d).wait_send()
-        for k in range(NZ):
-            pl.when(z != k)(lambda t=t, k=k: out_copy(t, k).wait_send())
+    arrive(stage_start, send_start)
+    arrive(stage_shells, send_shells)
+    pl.when(stays)(lambda: arrive(sums.at[pl.ds(0, PER - 1)], send_hop))
+    pl.when(jnp.logical_not(stays))(lambda: arrive(sums, send_hop))
+    arrive(hopped.at[:, pl.ds(0, (NZ - 1) * SHARE)], send_out)
+    arrive(out_ref, recv_out)
 
 
 def body(shells, start_values, rec_scale, rec_shift, rec_damp, degree_counts, owners):
@@ -302,14 +292,14 @@
             pltpu.VMEM((PER, NDEG, C), jnp.bfloat16),
             pltpu.VMEM((PER, NDEG, C), jnp.bfloat16),
             dma,
-            dma((NZ - 1,)),
-            dma((NZ - 1,)),
-            dma((NZ - 1, PER)),
-            dma((NZ - 1, PER)),
+            dma,
+            dma,
+            dma,
             dma((PER,)),
+            dma,
             dma((PER,)),
-            dma((PER, NZ)),
-            dma((GROUPS,)),
+            dma,
+            dma,
         ],
         compiler_params=pltpu.CompilerParams(
             collective_id=0, has_side_effects=True, vmem_limit_bytes=40 * 2**20

time: 48.6 us -> 47.4 us (0.975)
  Pallas kernels: 47.5 us -> 46.2 us
    pallas_call x1, Pallas kernels: 47.5 us -> 46.2 us  [body(): pl.pallas_call(kernel, out_shape=pltpu.VMEM((GROUPS, SHARE, C), jnp.bfloa...]
where the time goes in v5:
time: 47.4 us; the launch traced here: 47.3 us
  Pallas kernels  46.2 us (97%)
  other arithmetic  1.09 us (2%)
    pallas_call x1, Pallas kernels, body(): pl.pallas_call(kernel, out_shape=pltpu.VMEM((GROUPS, SHARE, C), jnp.bfloa...  46.2 us
    convert_element_type x1, other arithmetic, body(): return arrived.astype(jnp.float32)  1.09 us

profile of v5, /device:TPU:1, one launch (start us, length us, event | category | flops | bytes accessed | tf_op | source)
XLA Modules:
  0.0 47.3 jit_solution(13319721477384367433)
XLA Ops:
  0.0 46.2 %transform.1 = bf16[32,64,128]{2,1,0:T(8,128)(2,1)S(1)} custom-call(s32[32]{0:T(128)} %owners_hbm.1, s32[32]{0:T(128)} %counts_hbm.1, bf16[32,128,128]{2,1,0:T(8,128)(2,1)} %shells_hbm.1, f32[32,128]{1,0:T(8,128)} %start_hbm.1, f32[32,512]{1,0:T(8,128)} %scale_hbm.1, f32[32,512]{1,0:T(8,128)} %shift_hbm.1, f32[32,512]{1,0:T(8,128)} %damp_hbm.1), custom_call_target="tpu_custom_call" | custom-call | tf_op jit(solution)/shard_map/transform/pallas_call | solution.py:269
  46.2 1.1 %convert_element_type.3 = f32[32,64,128]{2,1,0:T(8,128)} convert(bf16[32,64,128]{2,1,0:T(8,128)(2,1)S(1)} %transform.1) | non-fusion elementwise | flops 262144 | bytes 1572864 | tf_op jit(solution)/shard_map/convert_element_type | solution.py:314

commit v6 on v5

--- a/solution.py
+++ b/solution.py
@@ -16,6 +16,7 @@
 SHARE = NDEG // NZ
 STEPS = (2, 3, 1, 0)
 HOME = 3
+PIECES = 8
 
 
 def ell_index(x, y, core):
@@ -49,6 +50,20 @@
 
     def device(to_e, to_z):
         return {"ell": to_e, "rad": to_z}
+
+    barrier = pltpu.get_barrier_semaphore()
+    for d in range(1, NZ):
+        pl.semaphore_signal(barrier, inc=1, device_id=device(e, lax.rem(z + d, NZ)), device_id_type=MESH)
+    stays = z == 0
+    for t in range(PER):
+
+        def greet(t=t):
+            pl.semaphore_signal(barrier, inc=1, device_id=device(group_of(e, z, t), z), device_id_type=MESH)
+
+        if t == HOME:
+            pl.when(jnp.logical_not(stays))(greet)
+        else:
+            greet()
 
     parts = 4
     loads = [
@@ -73,20 +88,6 @@
     ]
     for load in loads:
         load.start()
-
-    barrier = pltpu.get_barrier_semaphore()
-    for d in range(1, NZ):
-        pl.semaphore_signal(barrier, inc=1, device_id=device(e, lax.rem(z + d, NZ)), device_id_type=MESH)
-    stays = z == 0
-    for t in range(PER):
-
-        def greet(t=t):
-            pl.semaphore_signal(barrier, inc=1, device_id=device(group_of(e, z, t), z), device_id_type=MESH)
-
-        if t == HOME:
-            pl.when(jnp.logical_not(stays))(greet)
-        else:
-            greet()
 
     loads[0].wait()
     words = [jnp.int32(0)] * (GROUPS // 4)
@@ -261,6 +262,22 @@
     pl.when(jnp.logical_not(stays))(lambda: arrive(sums, send_hop))
     arrive(hopped.at[:, pl.ds(0, (NZ - 1) * SHARE)], send_out)
     arrive(out_ref, recv_out)
+
+
+def widen(short_ref, long_hbm, long, sems):
+    pieces = sems.shape[0]
+    part = GROUPS // pieces
+
+    def piece(i):
+        rows = pl.ds(i * part, part)
+        return pltpu.make_async_copy(long.at[rows], long_hbm.at[rows], sems.at[i])
+
+    for i in range(pieces):
+        rows = pl.ds(i * part, part)
+        long[rows] = short_ref[rows].astype(jnp.float32)
+        piece(i).start()
+    for i in range(pieces):
+        piece(i).wait()
 
 
 def body(shells, start_values, rec_scale, rec_shift, rec_damp, degree_counts, owners):
@@ -311,7 +328,15 @@
             for a in (owners, degree_counts, shells, start_values, rec_scale, rec_shift, rec_damp)
         )
     )
-    return arrived.astype(jnp.float32)
+    return pl.pallas_call(
+        widen,
+        out_shape=jax.ShapeDtypeStruct((GROUPS, SHARE, C), jnp.float32),
+        in_specs=[pl.BlockSpec(memory_space=pltpu.VMEM)],
+        out_specs=hbm,
+        scratch_shapes=[pltpu.VMEM((GROUPS, SHARE, C), jnp.float32), dma((PIECES,))],
+        compiler_params=pltpu.CompilerParams(vmem_limit_bytes=40 * 2**20),
+        name="widen",
+    )(arrived)
 
 
 def solution(mesh):

time: 47.4 us -> 47.3 us (level)
  other arithmetic: 1.09 us -> 0 us
  Pallas kernels: 46.2 us -> 47.1 us
    convert_element_type x1 -> x0, other arithmetic: 1.09 us -> none  [body(): return arrived.astype(jnp.float32)]
    pallas_call x0 -> x1, Pallas kernels: none -> 1.04 us  [body(): pl.pallas_call(widen, out_shape=jax.ShapeDtypeStruct((GROUPS, SHARE, C),...]
where the time goes in v6:
time: 47.3 us; the launch traced here: 47.2 us
  Pallas kernels  47.1 us (100%)
    pallas_call x1, Pallas kernels, body(): pl.pallas_call(kernel, out_shape=pltpu.VMEM((GROUPS, SHARE, C), jnp.bfloa...  46.1 us
    pallas_call x1, Pallas kernels, body(): pl.pallas_call(widen, out_shape=jax.ShapeDtypeStruct((GROUPS, SHARE, C),...  1.04 us

profile of v6, /device:TPU:1, one launch (start us, length us, event | category | flops | bytes accessed | tf_op | source)
XLA Modules:
  0.0 47.2 jit_solution(14543255420747737474)
XLA Ops:
  0.0 46.1 %transform.1.short_ref = bf16[32,64,128]{2,1,0:T(8,128)(2,1)S(1)} custom-call(s32[32]{0:T(128)} %owners_hbm.1, s32[32]{0:T(128)} %counts_hbm.1, bf16[32,128,128]{2,1,0:T(8,128)(2,1)} %shells_hbm.1, f32[32,128]{1,0:T(8,128)} %start_hbm.1, f32[32,512]{1,0:T(8,128)} %scale_hbm.1, f32[32,512]{1,0:T(8,128)} %shift_hbm.1, f32[32,512]{1,0:T(8,128)} %damp_hbm.1), custom_call_target="tpu_custom_call" | custom-call | tf_op jit(solution)/shard_map/transform/pallas_call | solution.py:286
  46.1 1.0 %widen.1 = f32[32,64,128]{2,1,0:T(8,128)} custom-call(bf16[32,64,128]{2,1,0:T(8,128)(2,1)S(1)} %transform.1.short_ref), custom_call_target="tpu_custom_call" | custom-call | tf_op jit(solution)/shard_map/widen/pallas_call | solution.py:331

commit v7 on v5

--- a/solution.py
+++ b/solution.py
@@ -49,6 +49,20 @@
 
     def device(to_e, to_z):
         return {"ell": to_e, "rad": to_z}
+
+    barrier = pltpu.get_barrier_semaphore()
+    for d in range(1, NZ):
+        pl.semaphore_signal(barrier, inc=1, device_id=device(e, lax.rem(z + d, NZ)), device_id_type=MESH)
+    stays = z == 0
+    for t in range(PER):
+
+        def greet(t=t):
+            pl.semaphore_signal(barrier, inc=1, device_id=device(group_of(e, z, t), z), device_id_type=MESH)
+
+        if t == HOME:
+            pl.when(jnp.logical_not(stays))(greet)
+        else:
+            greet()
 
     parts = 4
     loads = [
@@ -74,20 +88,6 @@
     for load in loads:
         load.start()
 
-    barrier = pltpu.get_barrier_semaphore()
-    for d in range(1, NZ):
-        pl.semaphore_signal(barrier, inc=1, device_id=device(e, lax.rem(z + d, NZ)), device_id_type=MESH)
-    stays = z == 0
-    for t in range(PER):
-
-        def greet(t=t):
-            pl.semaphore_signal(barrier, inc=1, device_id=device(group_of(e, z, t), z), device_id_type=MESH)
-
-        if t == HOME:
-            pl.when(jnp.logical_not(stays))(greet)
-        else:
-            greet()
-
     loads[0].wait()
     words = [jnp.int32(0)] * (GROUPS // 4)
     for p in range(GROUPS):
@@ -123,7 +123,7 @@
             device_id_type=MESH,
         )
 
-    far_first = (4, 3, 5, 2, 6, 1, 7)
+    far_first = (4, 5, 3, 6, 2, 7, 1)
     loads[1].wait()
     stage_start[...] = jnp.zeros_like(stage_start)
     to = [[order[owner_of(e, lax.rem(z + d, NZ), t)] for t in range(PER)] for d in range(NZ)]

time: 47.4 us -> 47.3 us (level)
  no operation moved by 1% of the time
where the time goes in v7:
time: 47.3 us; the launch traced here: 47.2 us
  Pallas kernels  46.1 us (97%)
  other arithmetic  1.09 us (2%)
    pallas_call x1, Pallas kernels, body(): pl.pallas_call(kernel, out_shape=pltpu.VMEM((GROUPS, SHARE, C), jnp.bfloa...  46.1 us
    convert_element_type x1, other arithmetic, body(): return arrived.astype(jnp.float32)  1.09 us

profile of v7, /device:TPU:1, one launch (start us, length us, event | category | flops | bytes accessed | tf_op | source)
XLA Modules:
  0.0 47.2 jit_solution(6159460477033805406)
XLA Ops:
  0.0 46.1 %transform.1 = bf16[32,64,128]{2,1,0:T(8,128)(2,1)S(1)} custom-call(s32[32]{0:T(128)} %owners_hbm.1, s32[32]{0:T(128)} %counts_hbm.1, bf16[32,128,128]{2,1,0:T(8,128)(2,1)} %shells_hbm.1, f32[32,128]{1,0:T(8,128)} %start_hbm.1, f32[32,512]{1,0:T(8,128)} %scale_hbm.1, f32[32,512]{1,0:T(8,128)} %shift_hbm.1, f32[32,512]{1,0:T(8,128)} %damp_hbm.1), custom_call_target="tpu_custom_call" | custom-call | tf_op jit(solution)/shard_map/transform/pallas_call | solution.py:269
  46.1 1.1 %convert_element_type.3 = f32[32,64,128]{2,1,0:T(8,128)} convert(bf16[32,64,128]{2,1,0:T(8,128)(2,1)S(1)} %transform.1) | non-fusion elementwise | flops 262144 | bytes 1572864 | tf_op jit(solution)/shard_map/convert_element_type | solution.py:314
